TPU v7x, 256 devices: a whole 4x4x8 slice. The times are simulated.
256 devices in a mesh: seq: 32 (over y_hi, z, core), grp: 8 (over y_lo, x).
Axes of the slice: x: 4, y: 4 (y_hi: 2, y_lo: 2; y = y_hi * 2 + y_lo), z: 8, core: 2. Of those that a mesh axis runs over, the one named last changes fastest.
Arguments:
- query_rows: bfloat16 [32768, 2048], P(('seq', 'grp')), may hold values from -24 to 24
- key_rows: bfloat16 [32768, 2048], P(('seq', 'grp')), may hold values from -24 to 24
- value_rows: bfloat16 [32768, 2048], P(('seq', 'grp')), may hold values from -8 to 8
- out_grad: bfloat16 [32768, 2048], P(('seq', 'grp')), may hold values from -6 to 6
Outputs:
- attended: bfloat16 [32768, 2048], P(('seq', 'grp'))
- query_grad: bfloat16 [32768, 2048], P(('seq', 'grp'))
- key_grad: bfloat16 [32768, 2048], P(('seq', 'grp'))
- value_grad: bfloat16 [32768, 2048], P(('seq', 'grp'))
All inputs are finite; a program needn't handle non-finite values.
Results may differ from a plain program's by a relative error of at most 0.034.
Values may be sent and summed in bfloat16 or wider, within the bound.
A program may use at most 128 MiB of HBM per device.

v0:
```python
import math

import jax
import jax.numpy as jnp
from jax import lax
from jax.sharding import PartitionSpec as P

E = 128
BLOCK = 128
LEVELS = 2


def from_behind(value, axis, steps):
    count = lax.axis_size(axis)
    leading, last = (max(0, -steps), min(count, count - steps))
    return lax.ppermute(value, axis, [(source, source + steps) for source in range(leading, last)])


def level_mask(height, query_pos, key_pos, key_count):
    key_block = jnp.floor_divide(key_pos, BLOCK)
    query_block = jnp.floor_divide(query_pos, BLOCK * 2**height)
    inside = (key_pos >= 0) & (key_pos < key_count)
    covered = inside[None, :] & (jnp.abs(key_block[None, :] - query_block[:, None]) <= 1)
    if height > 0:
        finer_block = jnp.floor_divide(query_pos, BLOCK * 2 ** (height - 1))
        pair_block = jnp.floor_divide(2 * key_pos, BLOCK)
        covered = covered & (jnp.abs(pair_block[None, :] - finer_block[:, None]) > 1)
    return covered


def pool_rows(stacked, height):
    if height == 0:
        return stacked
    factor = 2**height
    shaped = stacked.reshape(stacked.shape[0], stacked.shape[1] // factor, factor, stacked.shape[2])
    return jnp.mean(shaped.astype(jnp.float32), axis=2).astype(jnp.bfloat16)


def reach_rows(row_count):
    if row_count % BLOCK == 0:
        return BLOCK
    return 2 * BLOCK - math.gcd(row_count, BLOCK)


def send_near(sliced, offset):
    return from_behind(sliced, ("seq", "grp"), offset)


def send_home(sliced, offset):
    return from_behind(sliced, ("seq", "grp"), offset)


def assemble(stacked, margin, stride):
    row_count = stacked.shape[1]
    leading = []
    trailing = []
    filled = 0
    distance = 1
    while filled < margin:
        amount = min(row_count, margin - filled)
        leading.insert(0, send_near(stacked[:, row_count - amount :], distance * stride))
        trailing.append(send_near(stacked[:, :amount], -distance * stride))
        filled += amount
        distance += 1
    return jnp.concatenate(leading + [stacked] + trailing, axis=1)


def disperse(gradients, row_count, margin, stride):
    owned_rows = gradients[:, margin : margin + row_count]
    filled = 0
    distance = 1
    while filled < margin:
        amount = min(row_count, margin - filled)
        left_part = gradients[:, margin - filled - amount : margin - filled]
        right_part = gradients[
            :, margin + row_count + filled : margin + row_count + filled + amount
        ]
        from_right = send_home(left_part, -distance * stride)
        from_left = send_home(right_part, distance * stride)
        owned_rows = owned_rows.at[:, row_count - amount :].add(from_right)
        owned_rows = owned_rows.at[:, :amount].add(from_left)
        filled += amount
        distance += 1
    return owned_rows


def block_terms(query_part, grad_part, key_parts, value_parts, coverage):
    score_scale = E ** (-0.5)
    scores = []
    for height in range(len(key_parts)):
        raw_score = (
            jnp.einsum(
                "thd,khd->htk", query_part, key_parts[height], preferred_element_type=jnp.float32
            )
            * score_scale
        )
        scores.append(jnp.where(coverage[height][None], raw_score, -jnp.inf))
    peak_score = jnp.max(scores[0], axis=-1)
    for later_score in scores[1:]:
        peak_score = jnp.maximum(peak_score, jnp.max(later_score, axis=-1))
    weights = [
        2.0**height * jnp.exp(scores[height] - peak_score[..., None])
        for height in range(len(scores))
    ]
    totals = jnp.sum(weights[0], axis=-1)
    for later_weight in weights[1:]:
        totals = totals + jnp.sum(later_weight, axis=-1)
    chances = [entry / totals[..., None] for entry in weights]
    rounded = [entry.astype(jnp.bfloat16) for entry in chances]
    out_sum = jnp.einsum(
        "htk,khd->thd", rounded[0], value_parts[0], preferred_element_type=jnp.float32
    )
    for height in range(1, len(scores)):
        out_sum = out_sum + jnp.einsum(
            "htk,khd->thd", rounded[height], value_parts[height], preferred_element_type=jnp.float32
        )
    attended = out_sum.astype(jnp.bfloat16)
    row_dot = jnp.sum(grad_part.astype(jnp.float32) * attended.astype(jnp.float32), axis=-1).T
    query_grad = None
    key_grads = []
    value_grads = []
    for height in range(len(scores)):
        products = jnp.einsum(
            "thd,khd->htk", grad_part, value_parts[height], preferred_element_type=jnp.float32
        )
        slopes = (chances[height] * (products - row_dot[..., None])).astype(jnp.bfloat16)
        term = jnp.einsum(
            "htk,khd->thd", slopes, key_parts[height], preferred_element_type=jnp.float32
        )
        query_grad = term if query_grad is None else query_grad + term
        key_grads.append(
            jnp.einsum("htk,thd->khd", slopes, query_part, preferred_element_type=jnp.float32)
            * score_scale
        )
        value_grads.append(
            jnp.einsum(
                "htk,thd->khd", rounded[height], grad_part, preferred_element_type=jnp.float32
            )
        )
    return (attended, query_grad * score_scale, key_grads, value_grads)


def on_device(query_rows, key_rows, value_rows, out_grad):
    row_count, features = query_rows.shape
    seq_groups = lax.axis_size("grp")
    device_count = lax.axis_size("seq") * seq_groups
    position = lax.axis_index(("seq", "grp"))
    seq_total = row_count * device_count
    stacked = jnp.stack([key_rows, value_rows])
    windows = []
    firsts = []
    margins = []
    row_sizes = []
    for height in range(LEVELS):
        own_count = row_count // 2**height
        margin = reach_rows(own_count)
        windows.append(assemble(pool_rows(stacked, height), margin, 1))
        firsts.append(position * own_count - margin)
        margins.append(margin)
        row_sizes.append(own_count)
    coarse_rows = pool_rows(stacked, LEVELS)
    coarse_count = row_count // 2**LEVELS
    grouped = lax.all_gather(coarse_rows, "grp", axis=1, tiled=True)
    group_span = coarse_count * seq_groups
    margin = reach_rows(group_span)
    windows.append(assemble(grouped, margin, seq_groups))
    firsts.append(lax.axis_index("seq") * group_span - margin)
    margins.append(margin)
    row_sizes.append(group_span)
    head_count = features // E
    group_heads = math.gcd(head_count, 4)
    col_width = group_heads * E
    query_pos = position * row_count + jnp.arange(row_count, dtype=jnp.int32)
    coverage = [
        level_mask(
            height,
            query_pos,
            firsts[height] + jnp.arange(windows[height].shape[1], dtype=jnp.int32),
            seq_total // 2**height,
        )
        for height in range(LEVELS + 1)
    ]

    def one_group(group_at, partial_value):
        attended_acc, query_acc, gradients = partial_value
        column = group_at * col_width
        query_part = lax.dynamic_slice_in_dim(query_rows, column, col_width, 1).reshape(
            row_count, group_heads, E
        )
        grad_part = lax.dynamic_slice_in_dim(out_grad, column, col_width, 1).reshape(
            row_count, group_heads, E
        )
        key_parts = []
        value_parts = []
        for height in range(LEVELS + 1):
            window_cols = lax.dynamic_slice_in_dim(windows[height], column, col_width, 2)
            window_cols = window_cols.reshape(2, windows[height].shape[1], group_heads, E)
            key_parts.append(window_cols[0])
            value_parts.append(window_cols[1])
        attended, query_grad, key_grads, value_grads = block_terms(
            query_part, grad_part, key_parts, value_parts, coverage
        )
        attended_acc = lax.dynamic_update_slice_in_dim(
            attended_acc, attended.reshape(row_count, col_width), column, 1
        )
        query_acc = lax.dynamic_update_slice_in_dim(
            query_acc, query_grad.reshape(row_count, col_width), column, 1
        )
        new_grads = tuple(
            (
                lax.dynamic_update_slice_in_dim(
                    gradients[height],
                    jnp.stack([key_grads[height], value_grads[height]]).reshape(
                        2, windows[height].shape[1], col_width
                    ),
                    column,
                    2,
                )
                for height in range(LEVELS + 1)
            )
        )
        return (attended_acc, query_acc, new_grads)

    initial = (
        jnp.zeros((row_count, features), jnp.bfloat16),
        jnp.zeros((row_count, features), jnp.float32),
        tuple((jnp.zeros((2, entry.shape[1], features), jnp.float32) for entry in windows)),
    )
    attended, query_grad, gradients = lax.fori_loop(
        0, head_count // group_heads, one_group, initial
    )
    owned_levels = []
    for height in range(LEVELS):
        owned_levels.append(disperse(gradients[height], row_sizes[height], margins[height], 1))
    spread = disperse(gradients[LEVELS], row_sizes[LEVELS], margins[LEVELS], seq_groups)
    owned_levels.append(lax.psum_scatter(spread, "grp", scatter_dimension=1, tiled=True))
    combined = owned_levels[0]
    for height in range(1, LEVELS + 1):
        combined = combined + jnp.repeat(owned_levels[height] / 2.0**height, 2**height, axis=1)
    return (
        attended,
        query_grad.astype(jnp.bfloat16),
        combined[0].astype(jnp.bfloat16),
        combined[1].astype(jnp.bfloat16),
    )


def solution(mesh):
    placed = (
        P(("seq", "grp"), None),
        P(("seq", "grp"), None),
        P(("seq", "grp"), None),
        P(("seq", "grp"), None),
    )
    return jax.shard_map(
        on_device,
        mesh=mesh,
        in_specs=placed,
        out_specs=(
            P(("seq", "grp"), None),
            P(("seq", "grp"), None),
            P(("seq", "grp"), None),
            P(("seq", "grp"), None),
        ),
        check_vma=False,
    )
```

profile of v0, /device:TPU:107, one launch (start us, length us, event | category | flops | bytes accessed | tf_op | source)
XLA Modules:
  0.0 665.1 jit_solution(16050077868068233770)
XLA Ops:
  16.0 5.2 collective-permute-start.2
  21.2 4.0 collective-permute-start.3
  36.3 15.5 %collective-permute-start.7 = (bf16[2,64,2048]{2,1,0:T(8,128)(2,1)S(1)}, bf16[2,64,2048]{2,1,0:T(8,128)(2,1)S(1)}, u32[]{:S(2)}, u32[]{:S(2)}) collective-permute-start(bf16[2,64,2048]{2,1,0:T(8,128)(2,1)S(1)} %multiply_convert_fusion), channel_id=1, source_target_pairs={{3,0},{4,1},{5,2},{6,3},{7,4},{8,5},{9,6},{10,7},{11,8},{12,9},{13... | collective-permute-start | bytes 1572872 | tf_op jit(solution)/shard_map/ppermute | solution.py:16
  59.0 19.5 %collective-permute-start.1 = (bf16[2,128,2048]{1,2,0:T(8,128)(2,1)}, bf16[2,128,2048]{1,2,0:T(8,128)(2,1)}, u32[]{:S(2)}, u32[]{:S(2)}) collective-permute-start(bf16[2,128,2048]{1,2,0:T(8,128)(2,1)} %pad_maximum_fusion.4), channel_id=1, source_target_pairs={{1,0},{2,1},{3,2},{4,3},{5,4},{6,5},{7,6},{8,7},{9,8},{10,9},{11,1... | collective-permute-start | bytes 3145736 | tf_op jit(solution)/shard_map/ppermute | solution.py:16
  80.5 37.3 %all-gather.2.cloned.1.call-done = bf16[2,256,2048]{2,0,1:T(2,128)(2,1)} async-done(((bf16[2,32,2048]{2,0,1:T(2,128)(2,1)}), bf16[2,256,2048]{2,0,1:T(2,128)(2,1)}) %all-gather.2.cloned.1.call-update) | async-done | bytes 2097168 | tf_op jit(solution)/shard_map/all_gather | solution.py:163
  122.4 17.7 %collective-permute-start.9 = (bf16[2,128,2048]{2,0,1:T(2,128)(2,1)S(1)}, bf16[2,128,2048]{2,0,1:T(2,128)(2,1)S(1)}, u32[]{:S(2)}, u32[]{:S(2)}) collective-permute-start(bf16[2,128,2048]{2,0,1:T(2,128)(2,1)S(1)} %get-tuple-element.692), channel_id=1, source_target_pairs={{8,0},{9,1},{10,2},{11,3},{12,4},{13,5},{14,6},{15,7},{16,8},{17,9... | collective-permute-start | bytes 3145736 | tf_op jit(solution)/shard_map/ppermute | solution.py:16
  148.7 6.9 %pad_maximum_fusion.2 = bf16[2,512,2048]{2,0,1:T(2,128)(2,1)} fusion(bf16[2,128,2048]{2,0,1:T(2,128)(2,1)S(1)} %collective-permute-done.9, bf16[2,256,2048]{2,0,1:T(2,128)(2,1)S(1)} %copy-done.20, bf16[2,128,2048]{2,0,1:T(2,128)(2,1)S(1)} %collective-permute-done.8), kind=kLoop, calls=%fused_computation.80 | loop fusion | flops 4194304 | bytes 8388608 | tf_op jit(solution)/shard_map/concatenate | solution.py:65
  155.6 7.6 %broadcast_in_dim.134.clone = f32[2,512,2048]{2,0,1:T(2,128)} broadcast(f32[]{:T(128)} %constant.481.clone.1), dimensions={} | broadcast | bytes 8388612 | tf_op jit(solution)/shard_map/broadcast_in_dim | solution.py:227
  163.2 3.8 broadcast_in_dim.133
  172.1 184.6 %while.41 = (s32[]{:T(128)}, bf16[128,2048]{1,0:T(8,128)(2,1)}, bf16[128,2048]{1,0:T(8,128)(2,1)}, f32[2,384,2048]{2,1,0:T(8,128)}, f32[2,448,2048]{2,1,0:T(8,12...) while((s32[]{:T(128)}, bf16[128,2048]{1,0:T(8,128)(2,1)}, ...), condition=%wide.region_10.11_spmd.clone.clone, body=%wide.region_2.10_spmd.clone.clone.sunk | while | flops 1073904128 | bytes 125512648 | solution.py:229
  176.8 4.1 constant_dynamic-slice_fusion.14
  222.8 4.1 constant_dynamic-slice_fusion.14
  269.0 4.1 constant_dynamic-slice_fusion.14
  315.1 4.2 constant_dynamic-slice_fusion.14
  339.9 3.8 constant_dynamic-update-slice_fusion.16
  356.8 4.4 fusion.82
  367.9 3.9 slice.314
  371.9 17.8 %collective-permute-done.18 = f32[2,128,2048]{2,0,1:T(2,128)S(1)} collective-permute-done((f32[2,128,2048]{2,0,1:T(2,128)S(1)}, f32[2,128,2048]{2,0,1:T(2,128)S(1)}, u32[]{:S(2)}, u32[]{:S(2)}) %collective-permute-start.18) | collective-permute-done | bytes 2097184 | tf_op jit(solution)/shard_map/ppermute | solution.py:16
  392.9 4.8 fusion.51
  397.8 4.9 fusion.83
  408.9 6.3 collective-permute-start.14
  415.2 5.6 collective-permute-start.15
  422.8 36.6 %collective-permute-done.12 = f32[2,64,2048]{2,1,0:T(8,128)S(1)} collective-permute-done((f32[2,64,2048]{2,1,0:T(8,128)S(1)}, f32[2,64,2048]{2,1,0:T(8,128)S(1)}, u32[]{:S(2)}, u32[]{:S(2)}) %collective-permute-start.12) | collective-permute-done | bytes 1048608 | tf_op jit(solution)/shard_map/ppermute | solution.py:16
  459.4 5.1 collective-permute-start.17
  466.8 8.5 %collective-permute-start.10 = (f32[2,128,2048]{2,1,0:T(8,128)}, f32[2,128,2048]{2,1,0:T(8,128)}, u32[]{:S(2)}, u32[]{:S(2)}) collective-permute-start(f32[2,128,2048]{2,1,0:T(8,128)} %get-tuple-element.689), channel_id=1, source_target_pairs={{1,0},{2,1},{3,2},{4,3},{5,4},{6,5},{7,6},{8,7},{9,8},{10,9},{11,1... | collective-permute-start | bytes 6291464 | tf_op jit(solution)/shard_map/ppermute | solution.py:16
  475.3 21.8 %collective-permute-done.14 = f32[2,64,2048]{2,1,0:T(8,128)S(1)} collective-permute-done((f32[2,64,2048]{2,1,0:T(8,128)S(1)}, f32[2,64,2048]{2,1,0:T(8,128)S(1)}, u32[]{:S(2)}, u32[]{:S(2)}) %collective-permute-start.14) | collective-permute-done | bytes 1048608 | tf_op jit(solution)/shard_map/ppermute | solution.py:16
  501.5 7.1 %collective-permute-done.15 = f32[2,64,2048]{2,1,0:T(8,128)} collective-permute-done((f32[2,64,2048]{2,1,0:T(8,128)}, f32[2,64,2048]{2,1,0:T(8,128)}, u32[]{:S(2)}, u32[]{:S(2)}) %collective-permute-start.15) | collective-permute-done | bytes 1048608 | tf_op jit(solution)/shard_map/ppermute | solution.py:16
  508.6 20.0 %collective-permute-done.16 = f32[2,64,2048]{2,1,0:T(8,128)} collective-permute-done((f32[2,64,2048]{2,1,0:T(8,128)}, f32[2,64,2048]{2,1,0:T(8,128)}, u32[]{:S(2)}, u32[]{:S(2)}) %collective-permute-start.16) | collective-permute-done | bytes 1048608 | tf_op jit(solution)/shard_map/ppermute | solution.py:16
  528.6 7.8 %collective-permute-done.17 = f32[2,64,2048]{2,1,0:T(8,128)} collective-permute-done((f32[2,64,2048]{2,1,0:T(8,128)S(1)}, f32[2,64,2048]{2,1,0:T(8,128)}, u32[]{:S(2)}, u32[]{:S(2)}) %collective-permute-start.17) | collective-permute-done | bytes 1048608 | tf_op jit(solution)/shard_map/ppermute | solution.py:16
  536.4 3.8 add_multiply_fusion
  543.9 104.2 %all-reduce.3.cloned.1.call-done = f32[2,256,2048]{2,0,1:T(2,128)} async-done(((f32[2,256,2048]{2,0,1:T(2,128)}), f32[2,256,2048]{2,0,1:T(2,128)}) %all-reduce.3.cloned.1.call-update) | async-done | bytes 4194320
  651.8 5.0 add_convert_fusion
  (651 shorter events, 240.8 us)
Async XLA Ops:
  7.2 110.6 %all-gather.2.cloned.1.call-start = ((), (), s32[]{:S(2)}) async-start(), calls=%async_computation | async-start | bytes 2359296 | tf_op jit(solution)/shard_map/all_gather | solution.py:163
  12.3 635.7 %all-reduce.3.cloned.1.call-start = ((), (), s32[]{:S(2)}) async-start(), calls=%async_computation.1 | async-start | bytes 8388608
  16.0 20.3 %collective-permute-start.2 = (bf16[2,64,2048]{2,1,0:T(8,128)(2,1)S(1)}, bf16[2,64,2048]{2,1,0:T(8,128)(2,1)}, u32[]{:S(2)}, u32[]{:S(2)}) collective-permute-start(bf16[2,64,2048]{2,1,0:T(8,128)(2,1)S(1)} %multiply_convert_fusion), channel_id=1, source_target_pairs={{0,3},{1,4},{2,5},{3,6},{4,7},{5,8},{6,9},{7,10},{8,11},{9,12},{10... | collective-permute-start | bytes 1572872 | tf_op jit(solution)/shard_map/ppermute | solution.py:16
  21.2 32.6 %collective-permute-start.3 = (bf16[2,64,2048]{2,1,0:T(8,128)(2,1)S(1)}, bf16[2,64,2048]{2,1,0:T(8,128)(2,1)}, u32[]{:S(2)}, u32[]{:S(2)}) collective-permute-start(bf16[2,64,2048]{2,1,0:T(8,128)(2,1)S(1)} %multiply_convert_fusion), channel_id=1, source_target_pairs={{0,2},{1,3},{2,4},{3,5},{4,6},{5,7},{6,8},{7,9},{8,10},{9,11},{10,... | collective-permute-start | bytes 1572872 | tf_op jit(solution)/shard_map/ppermute | solution.py:16
  25.2 33.8 %collective-permute-start.4 = (bf16[2,64,2048]{2,1,0:T(8,128)(2,1)S(1)}, bf16[2,64,2048]{2,1,0:T(8,128)(2,1)}, u32[]{:S(2)}, u32[]{:S(2)}) collective-permute-start(bf16[2,64,2048]{2,1,0:T(8,128)(2,1)S(1)} %multiply_convert_fusion), channel_id=1, source_target_pairs={{0,1},{1,2},{2,3},{3,4},{4,5},{5,6},{6,7},{7,8},{8,9},{9,10},{10,1... | collective-permute-start | bytes 1572872 | tf_op jit(solution)/shard_map/ppermute | solution.py:16
  28.9 91.5 %collective-permute-start.5 = (bf16[2,64,2048]{2,1,0:T(8,128)(2,1)S(1)}, bf16[2,64,2048]{2,1,0:T(8,128)(2,1)}, u32[]{:S(2)}, u32[]{:S(2)}) collective-permute-start(bf16[2,64,2048]{2,1,0:T(8,128)(2,1)S(1)} %multiply_convert_fusion), channel_id=1, source_target_pairs={{1,0},{2,1},{3,2},{4,3},{5,4},{6,5},{7,6},{8,7},{9,8},{10,9},{11,1... | collective-permute-start | bytes 1572872 | tf_op jit(solution)/shard_map/ppermute | solution.py:16
  30.9 91.5 %collective-permute-start.6 = (bf16[2,64,2048]{2,1,0:T(8,128)(2,1)S(1)}, bf16[2,64,2048]{2,1,0:T(8,128)(2,1)}, u32[]{:S(2)}, u32[]{:S(2)}) collective-permute-start(bf16[2,64,2048]{2,1,0:T(8,128)(2,1)S(1)} %multiply_convert_fusion), channel_id=1, source_target_pairs={{2,0},{3,1},{4,2},{5,3},{6,4},{7,5},{8,6},{9,7},{10,8},{11,9},{12,... | collective-permute-start | bytes 1572872 | tf_op jit(solution)/shard_map/ppermute | solution.py:16
  36.3 108.5 %collective-permute-start.7 = (bf16[2,64,2048]{2,1,0:T(8,128)(2,1)S(1)}, bf16[2,64,2048]{2,1,0:T(8,128)(2,1)S(1)}, u32[]{:S(2)}, u32[]{:S(2)}) collective-permute-start(bf16[2,64,2048]{2,1,0:T(8,128)(2,1)S(1)} %multiply_convert_fusion), channel_id=1, source_target_pairs={{3,0},{4,1},{5,2},{6,3},{7,4},{8,5},{9,6},{10,7},{11,8},{12,9},{13... | collective-permute-start | bytes 1572872 | tf_op jit(solution)/shard_map/ppermute | solution.py:16
  53.7 91.9 %collective-permute-start = (bf16[2,128,2048]{1,2,0:T(8,128)(2,1)}, bf16[2,128,2048]{1,2,0:T(8,128)(2,1)}, u32[]{:S(2)}, u32[]{:S(2)}) collective-permute-start(bf16[2,128,2048]{1,2,0:T(8,128)(2,1)} %pad_maximum_fusion.4), channel_id=1, source_target_pairs={{0,1},{1,2},{2,3},{3,4},{4,5},{5,6},{6,7},{7,8},{8,9},{9,10},{10,1... | collective-permute-start | bytes 3145736 | tf_op jit(solution)/shard_map/ppermute | solution.py:16
  59.0 86.6 %collective-permute-start.1 = (bf16[2,128,2048]{1,2,0:T(8,128)(2,1)}, bf16[2,128,2048]{1,2,0:T(8,128)(2,1)}, u32[]{:S(2)}, u32[]{:S(2)}) collective-permute-start(bf16[2,128,2048]{1,2,0:T(8,128)(2,1)} %pad_maximum_fusion.4), channel_id=1, source_target_pairs={{1,0},{2,1},{3,2},{4,3},{5,4},{6,5},{7,6},{8,7},{9,8},{10,9},{11,1... | collective-permute-start | bytes 3145736 | tf_op jit(solution)/shard_map/ppermute | solution.py:16
  120.5 28.2 %collective-permute-start.8 = (bf16[2,128,2048]{2,0,1:T(2,128)(2,1)S(1)}, bf16[2,128,2048]{2,0,1:T(2,128)(2,1)S(1)}, u32[]{:S(2)}, u32[]{:S(2)}) collective-permute-start(bf16[2,128,2048]{2,0,1:T(2,128)(2,1)S(1)} %get-tuple-element.691), channel_id=1, source_target_pairs={{0,8},{1,9},{2,10},{3,11},{4,12},{5,13},{6,14},{7,15},{8,16},{9,17... | collective-permute-start | bytes 3145736 | tf_op jit(solution)/shard_map/ppermute | solution.py:16
  122.4 26.3 %collective-permute-start.9 = (bf16[2,128,2048]{2,0,1:T(2,128)(2,1)S(1)}, bf16[2,128,2048]{2,0,1:T(2,128)(2,1)S(1)}, u32[]{:S(2)}, u32[]{:S(2)}) collective-permute-start(bf16[2,128,2048]{2,0,1:T(2,128)(2,1)S(1)} %get-tuple-element.692), channel_id=1, source_target_pairs={{8,0},{9,1},{10,2},{11,3},{12,4},{13,5},{14,6},{15,7},{16,8},{17,9... | collective-permute-start | bytes 3145736 | tf_op jit(solution)/shard_map/ppermute | solution.py:16
  172.2 12.8 %copy-start.34 = (s32[128]{0:T(128)}, s32[128]{0:T(128)S(1)}, u32[]{:S(2)}) copy-start(s32[128]{0:T(128)S(1)} %get-tuple-element.931) | copy-start | bytes 1540 | tf_op jit(solution)/shard_map/while
  172.2 12.8 %copy-start.41 = (pred[384]{0:T(512)(128)(4,1)}, pred[384]{0:T(512)(128)(4,1)S(1)}, u32[]{:S(2)}) copy-start(pred[384]{0:T(512)(128)(4,1)S(1)} %get-tuple-element.933) | copy-start | bytes 1156 | tf_op jit(solution)/shard_map/while
  218.2 12.8 %copy-start.34 = (s32[128]{0:T(128)}, s32[128]{0:T(128)S(1)}, u32[]{:S(2)}) copy-start(s32[128]{0:T(128)S(1)} %get-tuple-element.931) | copy-start | bytes 1540 | tf_op jit(solution)/shard_map/while
  218.2 12.8 %copy-start.41 = (pred[384]{0:T(512)(128)(4,1)}, pred[384]{0:T(512)(128)(4,1)S(1)}, u32[]{:S(2)}) copy-start(pred[384]{0:T(512)(128)(4,1)S(1)} %get-tuple-element.933) | copy-start | bytes 1156 | tf_op jit(solution)/shard_map/while
  310.5 12.9 %copy-start.34 = (s32[128]{0:T(128)}, s32[128]{0:T(128)S(1)}, u32[]{:S(2)}) copy-start(s32[128]{0:T(128)S(1)} %get-tuple-element.931) | copy-start | bytes 1540 | tf_op jit(solution)/shard_map/while
  310.5 12.9 %copy-start.41 = (pred[384]{0:T(512)(128)(4,1)}, pred[384]{0:T(512)(128)(4,1)S(1)}, u32[]{:S(2)}) copy-start(pred[384]{0:T(512)(128)(4,1)S(1)} %get-tuple-element.933) | copy-start | bytes 1156 | tf_op jit(solution)/shard_map/while
  361.1 28.6 %collective-permute-start.18 = (f32[2,128,2048]{2,0,1:T(2,128)S(1)}, f32[2,128,2048]{2,0,1:T(2,128)S(1)}, u32[]{:S(2)}, u32[]{:S(2)}) collective-permute-start(f32[2,128,2048]{2,0,1:T(2,128)S(1)} %get-tuple-element.682), channel_id=1, source_target_pairs={{8,0},{9,1},{10,2},{11,3},{12,4},{13,5},{14,6},{15,7},{16,8},{17,9... | collective-permute-start | bytes 6291464 | tf_op jit(solution)/shard_map/ppermute | solution.py:16
  364.8 28.1 %collective-permute-start.19 = (f32[2,128,2048]{2,0,1:T(2,128)S(1)}, f32[2,128,2048]{2,0,1:T(2,128)S(1)}, u32[]{:S(2)}, u32[]{:S(2)}) collective-permute-start(f32[2,128,2048]{2,0,1:T(2,128)S(1)} %get-tuple-element.681), channel_id=1, source_target_pairs={{0,8},{1,9},{2,10},{3,11},{4,12},{5,13},{6,14},{7,15},{8,16},{9,17... | collective-permute-start | bytes 6291464 | tf_op jit(solution)/shard_map/ppermute | solution.py:16
  397.7 66.8 %slice-start = ((s8[6291456]{0:T(1024)(128)(4,1)}), s8[2097152]{0:T(1024)(128)(4,1)S(1)}, s32[]{:S(2)}) async-start(s8[6291456]{0:T(1024)(128)(4,1)} %bitcast.163), calls=%async_computation.2 | async-start | bytes 4194304
  397.8 66.7 %slice-start.1 = ((s8[6291456]{0:T(1024)(128)(4,1)}), s8[4194304]{0:T(1024)(128)(4,1)S(1)}, s32[]{:S(2)}) async-start(s8[6291456]{0:T(1024)(128)(4,1)} %bitcast.163), calls=%async_computation.3 | async-start | bytes 8388608
  402.6 56.8 %collective-permute-start.12 = (f32[2,64,2048]{2,1,0:T(8,128)S(1)}, f32[2,64,2048]{2,1,0:T(8,128)S(1)}, u32[]{:S(2)}, u32[]{:S(2)}) collective-permute-start(f32[2,64,2048]{2,1,0:T(8,128)S(1)} %get-tuple-element.683), channel_id=1, source_target_pairs={{1,0},{2,1},{3,2},{4,3},{5,4},{6,5},{7,6},{8,7},{9,8},{10,9},{11,1... | collective-permute-start | bytes 3145736 | tf_op jit(solution)/shard_map/ppermute | solution.py:16
  405.5 61.3 %collective-permute-start.13 = (f32[2,64,2048]{2,1,0:T(8,128)S(1)}, f32[2,64,2048]{2,1,0:T(8,128)S(1)}, u32[]{:S(2)}, u32[]{:S(2)}) collective-permute-start(f32[2,64,2048]{2,1,0:T(8,128)S(1)} %get-tuple-element.686), channel_id=1, source_target_pairs={{0,1},{1,2},{2,3},{3,4},{4,5},{5,6},{6,7},{7,8},{8,9},{9,10},{10,1... | collective-permute-start | bytes 3145736 | tf_op jit(solution)/shard_map/ppermute | solution.py:16
  408.9 88.2 %collective-permute-start.14 = (f32[2,64,2048]{2,1,0:T(8,128)S(1)}, f32[2,64,2048]{2,1,0:T(8,128)S(1)}, u32[]{:S(2)}, u32[]{:S(2)}) collective-permute-start(f32[2,64,2048]{2,1,0:T(8,128)S(1)} %get-tuple-element.685), channel_id=1, source_target_pairs={{2,0},{3,1},{4,2},{5,3},{6,4},{7,5},{8,6},{9,7},{10,8},{11,9},{12,... | collective-permute-start | bytes 3145736 | tf_op jit(solution)/shard_map/ppermute | solution.py:16
  415.2 93.4 %collective-permute-start.15 = (f32[2,64,2048]{2,1,0:T(8,128)}, f32[2,64,2048]{2,1,0:T(8,128)}, u32[]{:S(2)}, u32[]{:S(2)}) collective-permute-start(f32[2,64,2048]{2,1,0:T(8,128)} %get-tuple-element.684), channel_id=1, source_target_pairs={{0,2},{1,3},{2,4},{3,5},{4,6},{5,7},{6,8},{7,9},{8,10},{9,11},{10,... | collective-permute-start | bytes 3145736 | tf_op jit(solution)/shard_map/ppermute | solution.py:16
  420.8 107.8 %collective-permute-start.16 = (f32[2,64,2048]{2,1,0:T(8,128)}, f32[2,64,2048]{2,1,0:T(8,128)}, u32[]{:S(2)}, u32[]{:S(2)}) collective-permute-start(f32[2,64,2048]{2,1,0:T(8,128)} %get-tuple-element.688), channel_id=1, source_target_pairs={{3,0},{4,1},{5,2},{6,3},{7,4},{8,5},{9,6},{10,7},{11,8},{12,9},{13... | collective-permute-start | bytes 3145736 | tf_op jit(solution)/shard_map/ppermute | solution.py:16
  459.4 77.0 %collective-permute-start.17 = (f32[2,64,2048]{2,1,0:T(8,128)S(1)}, f32[2,64,2048]{2,1,0:T(8,128)}, u32[]{:S(2)}, u32[]{:S(2)}) collective-permute-start(f32[2,64,2048]{2,1,0:T(8,128)S(1)} %get-tuple-element.687), channel_id=1, source_target_pairs={{0,3},{1,4},{2,5},{3,6},{4,7},{5,8},{6,9},{7,10},{8,11},{9,12},{10... | collective-permute-start | bytes 3145736 | tf_op jit(solution)/shard_map/ppermute | solution.py:16
  464.5 35.8 %copy-start.49 = (u32[256]{0:T(256)S(1)}, u32[256]{0:T(256)}, u32[]{:S(2)}) copy-start(u32[256]{0:T(256)} %constant.510) | copy-start | bytes 3076
  466.8 30.3 %copy-start.28 = (f32[2,64,2048]{2,1,0:T(8,128)}, f32[2,64,2048]{2,1,0:T(8,128)S(1)}, u32[]{:S(2)}) copy-start(f32[2,64,2048]{2,1,0:T(8,128)S(1)} %collective-permute-done.13) | copy-start | bytes 3145732
  466.8 185.0 %collective-permute-start.10 = (f32[2,128,2048]{2,1,0:T(8,128)}, f32[2,128,2048]{2,1,0:T(8,128)}, u32[]{:S(2)}, u32[]{:S(2)}) collective-permute-start(f32[2,128,2048]{2,1,0:T(8,128)} %get-tuple-element.689), channel_id=1, source_target_pairs={{1,0},{2,1},{3,2},{4,3},{5,4},{6,5},{7,6},{8,7},{9,8},{10,9},{11,1... | collective-permute-start | bytes 6291464 | tf_op jit(solution)/shard_map/ppermute | solution.py:16
  498.1 153.7 %collective-permute-start.11 = (f32[2,128,2048]{2,1,0:T(8,128)}, f32[2,128,2048]{2,1,0:T(8,128)}, u32[]{:S(2)}, u32[]{:S(2)}) collective-permute-start(f32[2,128,2048]{2,1,0:T(8,128)} %get-tuple-element.690), channel_id=1, source_target_pairs={{0,1},{1,2},{2,3},{3,4},{4,5},{5,6},{6,7},{7,8},{8,9},{9,10},{10,1... | collective-permute-start | bytes 6291464 | tf_op jit(solution)/shard_map/ppermute | solution.py:16
  (180 other events, 726.6 us)
Sparse Core Ops, SparseCore 0:
  12.4 105.2 all-gather.1
  397.9 250.0 all-reduce.2
where the time goes:
time: 674 us; the launch traced here: 665 us
  waiting for transfers between devices  254 us (38%)
  local copies, waits for them, and re-layouts  173 us (26%)
  starting transfers between devices  118 us (18%)
  matrix products  55.5 us (8%)
  other arithmetic  45.9 us (7%)
  between operations  15.6 us (2%)
    ppermute x20, starting transfers between devices, from_behind(): lax.ppermute(value, axis, [(source, source + steps) for source in range(l...  118 us
    ppermute x20, waiting for transfers between devices, from_behind(): lax.ppermute(value, axis, [(source, source + steps) for source in range(l...  113 us
    unnamed x3, waiting for transfers between devices  104 us
    all_gather x1, waiting for transfers between devices, on_device(): grouped = lax.all_gather(coarse_rows, 'grp', axis=1, tiled=True)  37.3 us
    dynamic_update_slice x16, local copies, waits for them, and re-layouts, one_group(): lax.dynamic_update_slice_in_dim(gradients[height], jnp.stack([key_grads[h...  32 us
    while x368, local copies, waits for them, and re-layouts  24.4 us
    slice x4, local copies, waits for them, and re-layouts, one_group(): key_parts.append(window_cols[0])  16.6 us
    slice x8, local copies, waits for them, and re-layouts, one_group(): value_parts.append(window_cols[1])  15.7 us
  transfers between devices with their start and end apart: 22, of which 9 were waited for; matrix products, arithmetic and copies ran while one was open for 7% of the time, Pallas kernels for 0%

commit v1 on v0

v1 whole, which is shorter than its diff:
```python
import functools
import math

import jax
import jax.numpy as jnp
from jax import lax
from jax.experimental import pallas as pl
from jax.experimental.pallas import tpu as pltpu
from jax.sharding import PartitionSpec as P

E = 128
T = 128
STAGES = 2
MESH = pl.DeviceIdType.MESH
NEG = -1e30
SCALE = E ** (-0.5)
LOG2E = 1.4426950408889634

L0 = {-1: 0, 0: 3, 1: 6, 2: 7, 3: 8, 4: 9, 5: 10, 6: 11, 7: 14, 8: 17}
L1 = {-1: 1, 0: 4, 1: 12, 2: 13, 3: 15, 4: 18}
L2 = {-1: 2, 0: 5, 1: 16, 2: 19}
TILES = 20


def own_tile(block):
    return 5 + block - 2 * ((8 - block) // 8) + 2 * (block // 7)


def rows_of(tile):
    if isinstance(tile, int):
        return pl.ds(tile * T, T)
    return pl.ds(pl.multiple_of(tile * T, T), T)


def nt(a, b):
    return lax.dot_general(a, b, (((1,), (1,)), ((), ())), preferred_element_type=jnp.float32)


def nn(a, b):
    return lax.dot_general(a, b, (((1,), (0,)), ((), ())), preferred_element_type=jnp.float32)


def pair_terms(pair, queries, grads, keys, values, bias_prev, bias_next):
    scores = nt(keys, queries)
    products = nt(values, grads)
    zero = jnp.zeros((T, T), jnp.bfloat16)
    chance_cols, slope_cols = [], []
    for half in range(2):
        low, high = (0, T // 2), (T // 2, T // 2)
        whole = (0, T)
        pieces = []
        for at in range(half, half + 3):
            bias = None
            if pair == 0 and at == 0:
                bias = bias_prev
            if pair == 1 and at == 3:
                bias = bias_next
            pieces.append((at, whole, 0, bias))
        pieces.append((4, low if half == 0 else whole, 1, bias_prev if pair == 0 else None))
        pieces.append((5, whole if half == 0 else high, 1, bias_next if pair == 1 else None))
        pieces.append((6, low if pair == 0 else whole, 2, bias_prev))
        pieces.append((7, whole if pair == 0 else high, 2, bias_next))
        lanes = slice(half * T, half * T + T)

        def part(array, piece):
            start = piece[0] * T + piece[1][0]
            return array[start : start + piece[1][1], lanes]

        peak = None
        for piece in pieces:
            top = jnp.max(part(scores, piece).reshape(-1, 8, T), axis=0)
            if piece[3] is not None:
                top = top + piece[3]
            peak = top if peak is None else jnp.maximum(peak, top)
        peak = jnp.max(peak, axis=0, keepdims=True) * (SCALE * LOG2E)
        weights = []
        total = None
        for piece in pieces:
            shift = peak - float(piece[2])
            if piece[3] is not None:
                shift = shift - piece[3]
            weight = jnp.exp2(part(scores, piece) * (SCALE * LOG2E) - shift)
            weights.append(weight)
            term = jnp.sum(weight.reshape(-1, 8, T), axis=0)
            total = term if total is None else total + term
        inverse = 1.0 / jnp.sum(total, axis=0, keepdims=True)
        row_dot = None
        chances = []
        for piece, weight in zip(pieces, weights):
            chance = weight * inverse
            chances.append(chance)
            term = jnp.sum((chance * part(products, piece)).reshape(-1, 8, T), axis=0)
            row_dot = term if row_dot is None else row_dot + term
        row_dot = jnp.sum(row_dot, axis=0, keepdims=True)
        chance_tiles, slope_tiles = [zero] * 8, [zero] * 8
        for piece, chance in zip(pieces, chances):
            slope = (chance * (part(products, piece) - row_dot)).astype(jnp.bfloat16)
            chance = chance.astype(jnp.bfloat16)
            if piece[1] != whole:
                blank = jnp.zeros((T // 2, T), jnp.bfloat16)
                if piece[1] == low:
                    chance = jnp.concatenate([chance, blank], axis=0)
                    slope = jnp.concatenate([slope, blank], axis=0)
                else:
                    chance = jnp.concatenate([blank, chance], axis=0)
                    slope = jnp.concatenate([blank, slope], axis=0)
            chance_tiles[piece[0]] = chance
            slope_tiles[piece[0]] = slope
        chance_cols.append(jnp.concatenate(chance_tiles, axis=0))
        slope_cols.append(jnp.concatenate(slope_tiles, axis=0))
    chance = jnp.concatenate(chance_cols, axis=1)
    slope = jnp.concatenate(slope_cols, axis=1)
    attended = nn(values.T, chance).astype(jnp.bfloat16).T
    query_grad = (nn(keys.T, slope) * SCALE).astype(jnp.bfloat16).T
    return attended, query_grad, nn(slope, queries), nn(chance, grads)


def kernel(groups, q_in, k_in, v_in, g_in, att_out, dq_out, dk_out, dv_out,
           kv, qg, acc, grad_send, grad_recv, result,
           in_send, in_recv, halo_send, halo_recv, back_send, back_recv, out_send, out_recv):
    seq = lax.axis_index("seq")
    me = lax.axis_index("grp")
    nxt = lax.rem(seq + 1, groups)
    prv = lax.rem(seq + groups - 1, groups)

    def peer(step):
        return lax.rem(me // 4 + step // 4, 2) * 4 + lax.rem(lax.rem(me, 4) + lax.rem(step, 4), 4)

    barrier = pltpu.get_barrier_semaphore()

    def greet(step, carry):
        pl.semaphore_signal(barrier, inc=1, device_id=(seq, peer(step)), device_id_type=MESH)
        return carry

    lax.fori_loop(1, 8, greet, 0)
    pl.semaphore_signal(barrier, inc=1, device_id=(nxt, me), device_id_type=MESH)
    pl.semaphore_signal(barrier, inc=1, device_id=(prv, me), device_id_type=MESH)
    pl.semaphore_wait(barrier, 9)

    inputs = (k_in, v_in, q_in, g_in)
    outputs = (att_out, dq_out, dk_out, dv_out)

    def columns(device, stage):
        return pl.ds(pl.multiple_of(device * (STAGES * E) + stage * E, E), E)

    def in_slot(stage, which, block):
        if which < 2:
            return kv.at[stage, which, rows_of(own_tile(block))]
        return qg.at[stage, which - 2, rows_of(block)]

    def in_copy(stage, which, step):
        other = peer(step)
        return pltpu.make_async_remote_copy(
            src_ref=inputs[which].at[:, columns(other, stage)],
            dst_ref=in_slot(stage, which, me),
            send_sem=in_send.at[stage, which, step],
            recv_sem=in_recv.at[stage, which, me],
            device_id=(seq, other),
            device_id_type=MESH,
        )

    def in_local(stage, which):
        return pltpu.make_async_copy(
            inputs[which].at[:, columns(me, stage)],
            in_slot(stage, which, me),
            in_recv.at[stage, which, me],
        )

    for stage in range(STAGES):
        for which in range(4):

            def send(step, carry):
                in_copy(stage, which, step).start()
                return carry

            lax.fori_loop(1, 8, send, 0)
            in_local(stage, which).start()

    def wait_in(stage, which):
        def wait(block, carry):
            slot = in_slot(stage, which, block)
            pltpu.make_async_copy(slot, slot, in_recv.at[stage, which, block]).wait()
            return carry

        lax.fori_loop(0, 8, wait, 0)

    down = lax.broadcasted_iota(jnp.int32, (384, 512), 0)
    along = lax.broadcasted_iota(jnp.int32, (384, 512), 1)
    pool = jnp.where(
        down < 256,
        jnp.where(along // 2 == down, 0.5, 0.0),
        jnp.where(along // 4 == down - 256, 0.25, 0.0),
    ).astype(jnp.bfloat16)
    along = lax.broadcasted_iota(jnp.int32, (512, 384), 1)
    down = lax.broadcasted_iota(jnp.int32, (512, 384), 0)
    unpool = jnp.where(
        along < 256,
        jnp.where(down // 2 == along, 0.5, 0.0),
        jnp.where(down // 4 == along - 256, 0.25, 0.0),
    ).astype(jnp.bfloat16)

    def quad_tiles(quad):
        fine = [L0[4 * quad + i] for i in range(4)]
        return fine, [L1[2 * quad], L1[2 * quad + 1], L2[quad]]

    def halo_copy(stage, side):
        source, target, device = ((14, 0, nxt), (3, 17, prv))[side]
        return pltpu.make_async_remote_copy(
            src_ref=kv.at[stage, :, pl.ds(source * T, 3 * T)],
            dst_ref=kv.at[stage, :, pl.ds(target * T, 3 * T)],
            send_sem=halo_send.at[stage, side],
            recv_sem=halo_recv.at[stage, side],
            device_id=(device, me),
            device_id_type=MESH,
        )

    def back_copy(stage, side):
        return pltpu.make_async_remote_copy(
            src_ref=grad_send.at[stage, side],
            dst_ref=grad_recv.at[stage, side],
            send_sem=back_send.at[stage, side],
            recv_sem=back_recv.at[stage, side],
            device_id=((prv, nxt)[side], me),
            device_id_type=MESH,
        )

    def out_copy(stage, which, step):
        other = peer(step)
        return pltpu.make_async_remote_copy(
            src_ref=result.at[stage, which, rows_of(other)],
            dst_ref=outputs[which].at[:, columns(me, stage)],
            send_sem=out_send.at[stage, which, step],
            recv_sem=out_recv.at[stage, which, me],
            device_id=(seq, other),
            device_id_type=MESH,
        )

    def send_out(stage, which):
        def send(step, carry):
            out_copy(stage, which, step).start()
            return carry

        lax.fori_loop(1, 8, send, 0)
        pltpu.make_async_copy(
            result.at[stage, which, rows_of(me)],
            outputs[which].at[:, columns(me, stage)],
            out_recv.at[stage, which, me],
        ).start()

    def prepare(stage):
        for which in range(2):
            wait_in(stage, which)
        for which in range(2):
            for quad in range(2):
                fine, coarse = quad_tiles(quad)
                rows = jnp.concatenate([kv[stage, which, rows_of(i)] for i in fine], axis=0)
                pooled = nn(pool, rows).astype(jnp.bfloat16)
                for at, tile in enumerate(coarse):
                    kv[stage, which, rows_of(tile)] = pooled[at * T : at * T + T]
        for side in range(2):
            halo_copy(stage, side).start()

    def compute(stage):
        acc[stage] = jnp.zeros(acc.shape[1:], jnp.float32)
        for which in range(2, 4):
            wait_in(stage, which)
        for side in range(2):
            halo_copy(stage, side).wait()

        def one_quad(quad, carry):
            bias_prev = jnp.where((seq == 0) & (quad == 0), NEG, 0.0)
            bias_next = jnp.where((seq == groups - 1) & (quad == 1), NEG, 0.0)
            for pair in range(2):
                names = []
                for table, at0, at1 in (
                    [(L0, 2 * pair + i, 4 + 2 * pair + i) for i in (-1, 0, 1, 2)]
                    + [(L1, pair + i, 2 + pair + i) for i in (-1, 1)]
                    + [(L2, i, 1 + i) for i in (-1, 1)]
                ):
                    first, second = table[at0], table[at1]
                    names.append(first + quad * (second - first))
                keys = jnp.concatenate([kv[stage, 0, rows_of(i)] for i in names], axis=0)
                values = jnp.concatenate([kv[stage, 1, rows_of(i)] for i in names], axis=0)
                rows = pl.ds(pl.multiple_of(quad * 512 + pair * 256, 256), 256)
                attended, query_grad, key_terms, value_terms = pair_terms(
                    pair, qg[stage, 0, rows], qg[stage, 1, rows], keys, values, bias_prev, bias_next
                )
                result[stage, 0, rows] = attended
                result[stage, 1, rows] = query_grad
                for at, tile in enumerate(names):
                    acc[stage, 0, rows_of(tile)] += key_terms[at * T : at * T + T]
                    acc[stage, 1, rows_of(tile)] += value_terms[at * T : at * T + T]
            return carry

        lax.fori_loop(0, 2, one_quad, 0)
        grad_send[stage, 0] = acc[stage, :, pl.ds(0, 3 * T)].astype(jnp.bfloat16)
        grad_send[stage, 1] = acc[stage, :, pl.ds(17 * T, 3 * T)].astype(jnp.bfloat16)
        for side in range(2):
            back_copy(stage, side).start()
        for which in range(2):
            send_out(stage, which)

    def finish(stage):
        for side in range(2):
            back_copy(stage, side).wait()
        acc[stage, :, pl.ds(14 * T, 3 * T)] += grad_recv[stage, 0].astype(jnp.float32)
        acc[stage, :, pl.ds(3 * T, 3 * T)] += grad_recv[stage, 1].astype(jnp.float32)
        for which in range(2):
            for quad in range(2):
                fine, coarse = quad_tiles(quad)
                total = jnp.concatenate([acc[stage, which, rows_of(i)] for i in fine], axis=0)
                pooled = jnp.concatenate([acc[stage, which, rows_of(i)] for i in coarse], axis=0)
                total = total + nn(unpool, pooled.astype(jnp.bfloat16))
                if which == 0:
                    total = total * SCALE
                result[stage, 2 + which, pl.ds(quad * 512, 512)] = total.astype(jnp.bfloat16)
            send_out(stage, 2 + which)

    prepare(0)
    compute(0)
    prepare(1)
    finish(0)
    compute(1)
    finish(1)

    for stage in range(STAGES):
        for which in range(4):

            def wait_sent(step, carry):
                in_copy(stage, which, step).wait_send()
                out_copy(stage, which, step).wait_send()
                return carry

            def wait_landed(block, carry):
                slot = outputs[which].at[:, columns(block, stage)]
                pltpu.make_async_copy(slot, slot, out_recv.at[stage, which, block]).wait()
                return carry

            lax.fori_loop(1, 8, wait_sent, 0)
            lax.fori_loop(0, 8, wait_landed, 0)


def on_device(query_rows, key_rows, value_rows, out_grad):
    groups = lax.axis_size("seq")
    shape = jax.ShapeDtypeStruct(query_rows.shape, jnp.bfloat16)
    anywhere = pl.BlockSpec(memory_space=pl.ANY)
    dma = pltpu.SemaphoreType.DMA
    return pl.pallas_call(
        functools.partial(kernel, groups),
        out_shape=(shape,) * 4,
        in_specs=[anywhere] * 4,
        out_specs=(anywhere,) * 4,
        scratch_shapes=[
            pltpu.VMEM((STAGES, 2, TILES * T, E), jnp.bfloat16),
            pltpu.VMEM((STAGES, 2, 8 * T, E), jnp.bfloat16),
            pltpu.VMEM((STAGES, 2, TILES * T, E), jnp.float32),
            pltpu.VMEM((STAGES, 2, 2, 3 * T, E), jnp.bfloat16),
            pltpu.VMEM((STAGES, 2, 2, 3 * T, E), jnp.bfloat16),
            pltpu.VMEM((STAGES, 4, 8 * T, E), jnp.bfloat16),
            dma((STAGES, 4, 8)),
            dma((STAGES, 4, 8)),
            dma((STAGES, 2)),
            dma((STAGES, 2)),
            dma((STAGES, 2)),
            dma((STAGES, 2)),
            dma((STAGES, 4, 8)),
            dma((STAGES, 4, 8)),
        ],
        compiler_params=pltpu.CompilerParams(
            collective_id=0, has_side_effects=True, vmem_limit_bytes=48 * 2**20
        ),
    )(query_rows, key_rows, value_rows, out_grad)


def solution(mesh):
    placed = P(("seq", "grp"), None)
    return jax.shard_map(
        on_device,
        mesh=mesh,
        in_specs=(placed,) * 4,
        out_specs=(placed,) * 4,
        check_vma=False,
    )
```

time: 674 us -> 76.8 us (0.11)
  the two profiles are of different devices: /device:TPU:107 before, /device:TPU:8 now
where the time goes in v1:
time: 76.8 us; the launch traced here: 76.6 us
  Pallas kernels  68.6 us (89%)
  local copies, waits for them, and re-layouts  7.33 us (10%)
    pallas_call x1, Pallas kernels, on_device(): pl.pallas_call(functools.partial(kernel, groups), out_shape=(shape,) * 4,...  68.6 us
    unnamed x12, local copies, waits for them, and re-layouts  7.33 us

profile of v1, /device:TPU:8, one launch (start us, length us, event | category | flops | bytes accessed | tf_op | source)
XLA Modules:
  0.0 76.6 jit_solution(14673448603138392865)
XLA Ops:
  0.6 0.0 copy-start
  0.6 1.0 %copy-done = bf16[128,2048]{1,0:T(8,128)(2,1)S(1)} copy-done((bf16[128,2048]{1,0:T(8,128)(2,1)S(1)}, bf16[128,2048]{1,0:T(8,128)(2,1)}, u32[]{:S(2)}) %copy-start) | copy-done | bytes 524312
  1.7 0.0 copy-start.1
  1.7 1.0 %copy-done.1 = bf16[128,2048]{1,0:T(8,128)(2,1)S(1)} copy-done((bf16[128,2048]{1,0:T(8,128)(2,1)S(1)}, bf16[128,2048]{1,0:T(8,128)(2,1)}, u32[]{:S(2)}) %copy-start.1) | copy-done | bytes 524312
  2.7 0.0 copy-start.2
  2.7 1.0 %copy-done.2 = bf16[128,2048]{1,0:T(8,128)(2,1)S(1)} copy-done((bf16[128,2048]{1,0:T(8,128)(2,1)S(1)}, bf16[128,2048]{1,0:T(8,128)(2,1)}, u32[]{:S(2)}) %copy-start.2) | copy-done | bytes 524312
  3.8 0.0 copy-start.3
  3.8 1.0 %copy-done.3 = bf16[128,2048]{1,0:T(8,128)(2,1)S(1)} copy-done((bf16[128,2048]{1,0:T(8,128)(2,1)S(1)}, bf16[128,2048]{1,0:T(8,128)(2,1)}, u32[]{:S(2)}) %copy-start.3) | copy-done | bytes 524312
  4.8 68.6 %shard_map.75 = (bf16[128,2048]{1,0:T(8,128)(2,1)S(1)}, bf16[128,2048]{1,0:T(8,128)(2,1)S(1)}, bf16[128,2048]{1,0:T(8,128)(2,1)S(1)}, bf16[128,2048]{1,0:T(8,128)(2,1)S(1)}) custom-call(bf16[128,2048]{1,0:T(8,128)(2,1)S(1)} %copy-done, bf16[128,2048]{1,0:T(8,128)(2,1)S(1)} %copy-done.1, bf16[128,2048]{1,0:T(8,128)(2,1)S(1)} %copy-done.2, ...), custom_call_target="tpu_custom_call" | custom-call | tf_op jit(solution)/shard_map/pallas_call | solution.py:348
  73.4 0.8 %copy.12 = bf16[128,2048]{1,0:T(8,128)(2,1)} copy(bf16[128,2048]{1,0:T(8,128)(2,1)S(1)} %get-tuple-element.8) | data formatting | bytes 1048576
  74.2 0.8 %copy.13 = bf16[128,2048]{1,0:T(8,128)(2,1)} copy(bf16[128,2048]{1,0:T(8,128)(2,1)S(1)} %get-tuple-element.9) | data formatting | bytes 1048576
  75.0 0.8 %copy.14 = bf16[128,2048]{1,0:T(8,128)(2,1)} copy(bf16[128,2048]{1,0:T(8,128)(2,1)S(1)} %get-tuple-element.10) | data formatting | bytes 1048576
  75.8 0.8 %copy.15 = bf16[128,2048]{1,0:T(8,128)(2,1)} copy(bf16[128,2048]{1,0:T(8,128)(2,1)S(1)} %get-tuple-element.11) | data formatting | bytes 1048576
Async XLA Ops:
  0.6 1.0 %copy-start = (bf16[128,2048]{1,0:T(8,128)(2,1)S(1)}, bf16[128,2048]{1,0:T(8,128)(2,1)}, u32[]{:S(2)}) copy-start(bf16[128,2048]{1,0:T(8,128)(2,1)} %q_in.1) | copy-start | bytes 1572868
  1.7 1.0 %copy-start.1 = (bf16[128,2048]{1,0:T(8,128)(2,1)S(1)}, bf16[128,2048]{1,0:T(8,128)(2,1)}, u32[]{:S(2)}) copy-start(bf16[128,2048]{1,0:T(8,128)(2,1)} %k_in.1) | copy-start | bytes 1572868
  2.7 1.0 %copy-start.2 = (bf16[128,2048]{1,0:T(8,128)(2,1)S(1)}, bf16[128,2048]{1,0:T(8,128)(2,1)}, u32[]{:S(2)}) copy-start(bf16[128,2048]{1,0:T(8,128)(2,1)} %v_in.1) | copy-start | bytes 1572868
  3.8 1.0 %copy-start.3 = (bf16[128,2048]{1,0:T(8,128)(2,1)S(1)}, bf16[128,2048]{1,0:T(8,128)(2,1)}, u32[]{:S(2)}) copy-start(bf16[128,2048]{1,0:T(8,128)(2,1)} %g_in.1) | copy-start | bytes 1572868

commit v2 on v1

--- a/solution.py
+++ b/solution.py
@@ -120,8 +120,14 @@
            in_send, in_recv, halo_send, halo_recv, back_send, back_recv, out_send, out_recv):
     seq = lax.axis_index("seq")
     me = lax.axis_index("grp")
-    nxt = lax.rem(seq + 1, groups)
-    prv = lax.rem(seq + groups - 1, groups)
+    upper = seq // (groups // 2)
+
+    def group(step):
+        other = lax.rem(seq + groups + step, groups)
+        crossing = lax.rem(upper + other // (groups // 2), 2)
+        return other, lax.rem(me + 4 * crossing, 8)
+
+    nxt, prv = group(1), group(-1)
 
     def peer(step):
         return lax.rem(me // 4 + step // 4, 2) * 4 + lax.rem(lax.rem(me, 4) + lax.rem(step, 4), 4)
@@ -133,15 +139,16 @@
         return carry
 
     lax.fori_loop(1, 8, greet, 0)
-    pl.semaphore_signal(barrier, inc=1, device_id=(nxt, me), device_id_type=MESH)
-    pl.semaphore_signal(barrier, inc=1, device_id=(prv, me), device_id_type=MESH)
+    pl.semaphore_signal(barrier, inc=1, device_id=nxt, device_id_type=MESH)
+    pl.semaphore_signal(barrier, inc=1, device_id=prv, device_id_type=MESH)
     pl.semaphore_wait(barrier, 9)
 
     inputs = (k_in, v_in, q_in, g_in)
     outputs = (att_out, dq_out, dk_out, dv_out)
 
     def columns(device, stage):
-        return pl.ds(pl.multiple_of(device * (STAGES * E) + stage * E, E), E)
+        place = lax.rem(device + 4 * upper, 8)
+        return pl.ds(pl.multiple_of(place * (STAGES * E) + stage * E, E), E)
 
     def in_slot(stage, which, block):
         if which < 2:
@@ -166,15 +173,16 @@
             in_recv.at[stage, which, me],
         )
 
-    for stage in range(STAGES):
-        for which in range(4):
-
-            def send(step, carry):
-                in_copy(stage, which, step).start()
-                return carry
-
-            lax.fori_loop(1, 8, send, 0)
-            in_local(stage, which).start()
+    def send_in(stage, which):
+        def send(step, carry):
+            in_copy(stage, which, step).start()
+            return carry
+
+        lax.fori_loop(1, 8, send, 0)
+        in_local(stage, which).start()
+
+    for which in range(3):
+        send_in(0, which)
 
     def wait_in(stage, which):
         def wait(block, carry):
@@ -210,7 +218,7 @@
             dst_ref=kv.at[stage, :, pl.ds(target * T, 3 * T)],
             send_sem=halo_send.at[stage, side],
             recv_sem=halo_recv.at[stage, side],
-            device_id=(device, me),
+            device_id=device,
             device_id_type=MESH,
         )
 
@@ -220,7 +228,7 @@
             dst_ref=grad_recv.at[stage, side],
             send_sem=back_send.at[stage, side],
             recv_sem=back_recv.at[stage, side],
-            device_id=((prv, nxt)[side], me),
+            device_id=(prv, nxt)[side],
             device_id_type=MESH,
         )
 
@@ -235,21 +243,29 @@
             device_id_type=MESH,
         )
 
-    def send_out(stage, which):
+    def send_out(stage, which, first=0, end=8):
         def send(step, carry):
-            out_copy(stage, which, step).start()
+            @pl.when(step != 0)
+            def _():
+                out_copy(stage, which, step).start()
+
+            @pl.when(step == 0)
+            def _():
+                pltpu.make_async_copy(
+                    result.at[stage, which, rows_of(me)],
+                    outputs[which].at[:, columns(me, stage)],
+                    out_recv.at[stage, which, me],
+                ).start()
+
             return carry
 
-        lax.fori_loop(1, 8, send, 0)
-        pltpu.make_async_copy(
-            result.at[stage, which, rows_of(me)],
-            outputs[which].at[:, columns(me, stage)],
-            out_recv.at[stage, which, me],
-        ).start()
+        lax.fori_loop(first, end, send, 0)
 
     def prepare(stage):
         for which in range(2):
             wait_in(stage, which)
+            if stage == 0:
+                send_in(which, 3 if which == 0 else 0)
         for which in range(2):
             for quad in range(2):
                 fine, coarse = quad_tiles(quad)
@@ -264,10 +280,15 @@
         acc[stage] = jnp.zeros(acc.shape[1:], jnp.float32)
         for which in range(2, 4):
             wait_in(stage, which)
+            if stage == 0:
+                send_in(1, which - 1)
+        if stage == 0:
+            send_in(1, 3)
         for side in range(2):
             halo_copy(stage, side).wait()
 
-        def one_quad(quad, carry):
+        def one_quad(turn):
+            quad = lax.rem(me // 4 + 1 + turn, 2)
             bias_prev = jnp.where((seq == 0) & (quad == 0), NEG, 0.0)
             bias_next = jnp.where((seq == groups - 1) & (quad == 1), NEG, 0.0)
             for pair in range(2):
@@ -290,15 +311,18 @@
                 for at, tile in enumerate(names):
                     acc[stage, 0, rows_of(tile)] += key_terms[at * T : at * T + T]
                     acc[stage, 1, rows_of(tile)] += value_terms[at * T : at * T + T]
+            for which in range(2):
+                send_out(stage, which, 4 - 4 * turn, 8 - 4 * turn)
+
+        def first_turn(turn, carry):
+            one_quad(turn)
             return carry
 
-        lax.fori_loop(0, 2, one_quad, 0)
+        lax.fori_loop(0, 2, first_turn, 0)
         grad_send[stage, 0] = acc[stage, :, pl.ds(0, 3 * T)].astype(jnp.bfloat16)
         grad_send[stage, 1] = acc[stage, :, pl.ds(17 * T, 3 * T)].astype(jnp.bfloat16)
         for side in range(2):
             back_copy(stage, side).start()
-        for which in range(2):
-            send_out(stage, which)
 
     def finish(stage):
         for side in range(2):
@@ -367,7 +391,7 @@
             dma((STAGES, 4, 8)),
         ],
         compiler_params=pltpu.CompilerParams(
-            collective_id=0, has_side_effects=True, vmem_limit_bytes=48 * 2**20
+            collective_id=0, has_side_effects=True, vmem_limit_bytes=63 * 2**20
         ),
     )(query_rows, key_rows, value_rows, out_grad)
 

time: 76.8 us -> 64.3 us (0.84)
  Pallas kernels: 68.6 us -> 58.1 us
  local copies, waits for them, and re-layouts: 7.33 us -> 5.19 us
    pallas_call x1, Pallas kernels: 68.6 us -> 58.1 us  [on_device(): pl.pallas_call(functools.partial(kernel, groups), out_shape=(shape,) * 4,...]
    unnamed x12 -> x10, local copies, waits for them, and re-layouts: 7.33 us -> 5.19 us
where the time goes in v2:
time: 64.3 us; the launch traced here: 64 us
  Pallas kernels  58.1 us (90%)
  local copies, waits for them, and re-layouts  5.19 us (8%)
  between operations  0.65 us (1%)
    pallas_call x1, Pallas kernels, on_device(): pl.pallas_call(functools.partial(kernel, groups), out_shape=(shape,) * 4,...  58.1 us
    unnamed x10, local copies, waits for them, and re-layouts  5.19 us

profile of v2, /device:TPU:8, one launch (start us, length us, event | category | flops | bytes accessed | tf_op | source)
XLA Modules:
  0.0 64.0 jit_solution(3579454632299713567)
XLA Ops:
  0.6 58.1 %shard_map.75 = (bf16[128,2048]{1,0:T(8,128)(2,1)}, bf16[128,2048]{1,0:T(8,128)(2,1)}, bf16[128,2048]{1,0:T(8,128)(2,1)}, bf16[128,2048]{1,0:T(8,128)(2,1)}) custom-call(bf16[128,2048]{1,0:T(8,128)(2,1)} %q_in.1, bf16[128,2048]{1,0:T(8,128)(2,1)} %k_in.1, bf16[128,2048]{1,0:T(8,128)(2,1)} %v_in.1, bf16[128,2048]{1,0:T(8,128)(2,1)} %g_in.1), custom_call_target="tpu_custom_call" | custom-call | tf_op jit(solution)/shard_map/pallas_call | solution.py:372
  58.8 0.0 copy-start.2
  58.8 1.9 %copy.12 = bf16[128,2048]{1,0:T(8,128)(2,1)} copy(bf16[128,2048]{1,0:T(8,128)(2,1)} %get-tuple-element.8) | data formatting | bytes 1048576
  60.7 0.0 copy-done.2
  60.7 0.0 copy-start.1
  60.7 0.8 %copy.13 = bf16[128,2048]{1,0:T(8,128)(2,1)} copy(bf16[128,2048]{1,0:T(8,128)(2,1)S(1)} %copy-done.2) | data formatting | bytes 1048576
  61.5 0.4 copy-done.1
  62.0 0.0 copy-start
  62.0 0.8 %copy.14 = bf16[128,2048]{1,0:T(8,128)(2,1)} copy(bf16[128,2048]{1,0:T(8,128)(2,1)S(1)} %copy-done.1) | data formatting | bytes 1048576
  62.8 0.4 copy-done
  63.2 0.8 %copy.15 = bf16[128,2048]{1,0:T(8,128)(2,1)} copy(bf16[128,2048]{1,0:T(8,128)(2,1)S(1)} %copy-done) | data formatting | bytes 1048576
Async XLA Ops:
  58.8 2.0 %copy-start.2 = (bf16[128,2048]{1,0:T(8,128)(2,1)S(1)}, bf16[128,2048]{1,0:T(8,128)(2,1)}, u32[]{:S(2)}) copy-start(bf16[128,2048]{1,0:T(8,128)(2,1)} %get-tuple-element.9) | copy-start | bytes 1572868
  60.7 1.2 %copy-start.1 = (bf16[128,2048]{1,0:T(8,128)(2,1)S(1)}, bf16[128,2048]{1,0:T(8,128)(2,1)}, u32[]{:S(2)}) copy-start(bf16[128,2048]{1,0:T(8,128)(2,1)} %get-tuple-element.10) | copy-start | bytes 1572868
  62.0 1.2 %copy-start = (bf16[128,2048]{1,0:T(8,128)(2,1)S(1)}, bf16[128,2048]{1,0:T(8,128)(2,1)}, u32[]{:S(2)}) copy-start(bf16[128,2048]{1,0:T(8,128)(2,1)} %get-tuple-element.11) | copy-start | bytes 1572868

commit v3 on v2

--- a/solution.py
+++ b/solution.py
@@ -74,7 +74,7 @@
             peak = top if peak is None else jnp.maximum(peak, top)
         peak = jnp.max(peak, axis=0, keepdims=True) * (SCALE * LOG2E)
         weights = []
-        total = None
+        total = row_dot = None
         for piece in pieces:
             shift = peak - float(piece[2])
             if piece[3] is not None:
@@ -83,17 +83,13 @@
             weights.append(weight)
             term = jnp.sum(weight.reshape(-1, 8, T), axis=0)
             total = term if total is None else total + term
+            term = jnp.sum((weight * part(products, piece)).reshape(-1, 8, T), axis=0)
+            row_dot = term if row_dot is None else row_dot + term
         inverse = 1.0 / jnp.sum(total, axis=0, keepdims=True)
-        row_dot = None
-        chances = []
+        row_dot = jnp.sum(row_dot, axis=0, keepdims=True) * inverse
+        chance_tiles, slope_tiles = [zero] * 8, [zero] * 8
         for piece, weight in zip(pieces, weights):
             chance = weight * inverse
-            chances.append(chance)
-            term = jnp.sum((chance * part(products, piece)).reshape(-1, 8, T), axis=0)
-            row_dot = term if row_dot is None else row_dot + term
-        row_dot = jnp.sum(row_dot, axis=0, keepdims=True)
-        chance_tiles, slope_tiles = [zero] * 8, [zero] * 8
-        for piece, chance in zip(pieces, chances):
             slope = (chance * (part(products, piece) - row_dot)).astype(jnp.bfloat16)
             chance = chance.astype(jnp.bfloat16)
             if piece[1] != whole:
@@ -364,12 +360,24 @@
             lax.fori_loop(0, 8, wait_landed, 0)
 
 
+def settle(*refs):
+    sources, targets, sem = refs[:4], refs[4:8], refs[8]
+    copies = [
+        pltpu.make_async_copy(source, target, sem.at[at])
+        for at, (source, target) in enumerate(zip(sources, targets))
+    ]
+    for copy in copies:
+        copy.start()
+    for copy in copies:
+        copy.wait()
+
+
 def on_device(query_rows, key_rows, value_rows, out_grad):
     groups = lax.axis_size("seq")
     shape = jax.ShapeDtypeStruct(query_rows.shape, jnp.bfloat16)
     anywhere = pl.BlockSpec(memory_space=pl.ANY)
     dma = pltpu.SemaphoreType.DMA
-    return pl.pallas_call(
+    moved = pl.pallas_call(
         functools.partial(kernel, groups),
         out_shape=(shape,) * 4,
         in_specs=[anywhere] * 4,
@@ -391,9 +399,17 @@
             dma((STAGES, 4, 8)),
         ],
         compiler_params=pltpu.CompilerParams(
-            collective_id=0, has_side_effects=True, vmem_limit_bytes=63 * 2**20
+            collective_id=0, has_side_effects=True, vmem_limit_bytes=413 * 2**17
         ),
     )(query_rows, key_rows, value_rows, out_grad)
+    return pl.pallas_call(
+        settle,
+        out_shape=(shape,) * 4,
+        in_specs=[anywhere] * 4,
+        out_specs=(anywhere,) * 4,
+        scratch_shapes=[dma((4,))],
+        compiler_params=pltpu.CompilerParams(vmem_limit_bytes=2**20),
+    )(*moved)
 
 
 def solution(mesh):

time: 64.3 us -> 59.9 us (0.932)
  local copies, waits for them, and re-layouts: 5.19 us -> 0 us
  Pallas kernels: 58.1 us -> 59.1 us
    unnamed x10 -> x0, local copies, waits for them, and re-layouts: 5.19 us -> none
    pallas_call x0 -> x1, Pallas kernels: none -> 1.35 us  [on_device(): pl.pallas_call(settle, out_shape=(shape,) * 4, in_specs=[anywhere] * 4, o...]
where the time goes in v3:
time: 59.9 us; the launch traced here: 59.7 us
  Pallas kernels  59.1 us (99%)
  between operations  0.64 us (1%)
    pallas_call x1, Pallas kernels, on_device(): pl.pallas_call(functools.partial(kernel, groups), out_shape=(shape,) * 4,...  57.7 us
    pallas_call x1, Pallas kernels, on_device(): pl.pallas_call(settle, out_shape=(shape,) * 4, in_specs=[anywhere] * 4, o...  1.35 us

profile of v3, /device:TPU:8, one launch (start us, length us, event | category | flops | bytes accessed | tf_op | source)
XLA Modules:
  0.0 59.7 jit_solution(12641425645273013712)
XLA Ops:
  0.6 57.7 %shard_map.75 = (bf16[128,2048]{1,0:T(8,128)(2,1)S(1)}, bf16[128,2048]{1,0:T(8,128)(2,1)S(1)}, bf16[128,2048]{1,0:T(8,128)(2,1)S(1)}, bf16[128,2048]{1,0:T(8,128)(2,1)S(1)}) custom-call(bf16[128,2048]{1,0:T(8,128)(2,1)} %q_in.1, bf16[128,2048]{1,0:T(8,128)(2,1)} %k_in.1, bf16[128,2048]{1,0:T(8,128)(2,1)} %v_in.1, bf16[128,2048]{1,0:T(8,128)(2,1)} %g_in.1), custom_call_target="tpu_custom_call" | custom-call | tf_op jit(solution)/shard_map/pallas_call | solution.py:380
  58.4 1.3 %shard_map.76 = (bf16[128,2048]{1,0:T(8,128)(2,1)}, bf16[128,2048]{1,0:T(8,128)(2,1)}, bf16[128,2048]{1,0:T(8,128)(2,1)}, bf16[128,2048]{1,0:T(8,128)(2,1)}) custom-call(bf16[128,2048]{1,0:T(8,128)(2,1)S(1)} %get-tuple-element.8.refs_0_, bf16[128,2048]{1,0:T(8,128)(2,1)S(1)} %get-tuple-element.9.refs_1_, bf16[128,2048]{1,0:T(8,128)(2,1)S(1)} %get-tuple-element.10.refs_2_, ...), custom_call_target="tpu_custom_call" | custom-call | tf_op jit(solution)/shard_map/pallas_call | solution.py:405

commit v4 on v3

--- a/solution.py
+++ b/solution.py
@@ -125,26 +125,26 @@
 
     nxt, prv = group(1), group(-1)
 
-    def peer(step):
-        return lax.rem(me // 4 + step // 4, 2) * 4 + lax.rem(lax.rem(me, 4) + lax.rem(step, 4), 4)
+    peers = [
+        lax.rem(me // 4 + step // 4, 2) * 4 + lax.rem(lax.rem(me, 4) + step % 4, 4)
+        for step in range(8)
+    ]
+    peers[0] = me
 
     barrier = pltpu.get_barrier_semaphore()
 
-    def greet(step, carry):
-        pl.semaphore_signal(barrier, inc=1, device_id=(seq, peer(step)), device_id_type=MESH)
-        return carry
-
-    lax.fori_loop(1, 8, greet, 0)
+    for other in peers[1:]:
+        pl.semaphore_signal(barrier, inc=1, device_id=(seq, other), device_id_type=MESH)
     pl.semaphore_signal(barrier, inc=1, device_id=nxt, device_id_type=MESH)
     pl.semaphore_signal(barrier, inc=1, device_id=prv, device_id_type=MESH)
     pl.semaphore_wait(barrier, 9)
 
     inputs = (k_in, v_in, q_in, g_in)
     outputs = (att_out, dq_out, dk_out, dv_out)
-
-    def columns(device, stage):
-        place = lax.rem(device + 4 * upper, 8)
-        return pl.ds(pl.multiple_of(place * (STAGES * E) + stage * E, E), E)
+    starts = [lax.rem(other + 4 * upper, 8) * (STAGES * E) for other in peers]
+
+    def columns(step, stage):
+        return pl.ds(pl.multiple_of(starts[step] + stage * E, E), E)
 
     def in_slot(stage, which, block):
         if which < 2:
@@ -152,41 +152,30 @@
         return qg.at[stage, which - 2, rows_of(block)]
 
     def in_copy(stage, which, step):
-        other = peer(step)
+        source = inputs[which].at[:, columns(step, stage)]
+        target = in_slot(stage, which, me)
+        if step == 0:
+            return pltpu.make_async_copy(source, target, in_recv.at[stage, which])
         return pltpu.make_async_remote_copy(
-            src_ref=inputs[which].at[:, columns(other, stage)],
-            dst_ref=in_slot(stage, which, me),
-            send_sem=in_send.at[stage, which, step],
-            recv_sem=in_recv.at[stage, which, me],
-            device_id=(seq, other),
+            src_ref=source,
+            dst_ref=target,
+            send_sem=in_send.at[stage, which],
+            recv_sem=in_recv.at[stage, which],
+            device_id=(seq, peers[step]),
             device_id_type=MESH,
         )
 
-    def in_local(stage, which):
-        return pltpu.make_async_copy(
-            inputs[which].at[:, columns(me, stage)],
-            in_slot(stage, which, me),
-            in_recv.at[stage, which, me],
-        )
-
     def send_in(stage, which):
-        def send(step, carry):
+        for step in (1, 2, 3, 4, 5, 6, 7, 0):
             in_copy(stage, which, step).start()
-            return carry
-
-        lax.fori_loop(1, 8, send, 0)
-        in_local(stage, which).start()
 
     for which in range(3):
         send_in(0, which)
+    acc[...] = jnp.zeros(acc.shape, jnp.float32)
 
     def wait_in(stage, which):
-        def wait(block, carry):
-            slot = in_slot(stage, which, block)
-            pltpu.make_async_copy(slot, slot, in_recv.at[stage, which, block]).wait()
-            return carry
-
-        lax.fori_loop(0, 8, wait, 0)
+        eight = qg.at[stage, 0]
+        pltpu.make_async_copy(eight, eight, in_recv.at[stage, which]).wait()
 
     down = lax.broadcasted_iota(jnp.int32, (384, 512), 0)
     along = lax.broadcasted_iota(jnp.int32, (384, 512), 1)
@@ -228,34 +217,22 @@
             device_id_type=MESH,
         )
 
-    def out_copy(stage, which, step):
-        other = peer(step)
-        return pltpu.make_async_remote_copy(
-            src_ref=result.at[stage, which, rows_of(other)],
-            dst_ref=outputs[which].at[:, columns(me, stage)],
-            send_sem=out_send.at[stage, which, step],
-            recv_sem=out_recv.at[stage, which, me],
-            device_id=(seq, other),
-            device_id_type=MESH,
-        )
-
-    def send_out(stage, which, first=0, end=8):
-        def send(step, carry):
-            @pl.when(step != 0)
-            def _():
-                out_copy(stage, which, step).start()
-
-            @pl.when(step == 0)
-            def _():
-                pltpu.make_async_copy(
-                    result.at[stage, which, rows_of(me)],
-                    outputs[which].at[:, columns(me, stage)],
-                    out_recv.at[stage, which, me],
+    def send_out(stage, part, steps):
+        for which in (2 * part, 2 * part + 1):
+            for step in steps:
+                source = result.at[stage, which, rows_of(peers[step])]
+                target = outputs[which].at[:, columns(0, stage)]
+                if step == 0:
+                    pltpu.make_async_copy(source, target, out_recv.at[stage, part]).start()
+                    continue
+                pltpu.make_async_remote_copy(
+                    src_ref=source,
+                    dst_ref=target,
+                    send_sem=out_send.at[stage, part],
+                    recv_sem=out_recv.at[stage, part],
+                    device_id=(seq, peers[step]),
+                    device_id_type=MESH,
                 ).start()
-
-            return carry
-
-        lax.fori_loop(first, end, send, 0)
 
     def prepare(stage):
         for which in range(2):
@@ -273,7 +250,6 @@
             halo_copy(stage, side).start()
 
     def compute(stage):
-        acc[stage] = jnp.zeros(acc.shape[1:], jnp.float32)
         for which in range(2, 4):
             wait_in(stage, which)
             if stage == 0:
@@ -307,14 +283,20 @@
                 for at, tile in enumerate(names):
                     acc[stage, 0, rows_of(tile)] += key_terms[at * T : at * T + T]
                     acc[stage, 1, rows_of(tile)] += value_terms[at * T : at * T + T]
-            for which in range(2):
-                send_out(stage, which, 4 - 4 * turn, 8 - 4 * turn)
-
-        def first_turn(turn, carry):
+
+            @pl.when(turn == 0)
+            def _():
+                send_out(stage, 0, (4, 5, 6, 7))
+
+            @pl.when(turn == 1)
+            def _():
+                send_out(stage, 0, (1, 2, 3, 0))
+
+        def next_turn(turn, carry):
             one_quad(turn)
             return carry
 
-        lax.fori_loop(0, 2, first_turn, 0)
+        lax.fori_loop(0, 2, next_turn, 0)
         grad_send[stage, 0] = acc[stage, :, pl.ds(0, 3 * T)].astype(jnp.bfloat16)
         grad_send[stage, 1] = acc[stage, :, pl.ds(17 * T, 3 * T)].astype(jnp.bfloat16)
         for side in range(2):
@@ -334,7 +316,7 @@
                 if which == 0:
                     total = total * SCALE
                 result[stage, 2 + which, pl.ds(quad * 512, 512)] = total.astype(jnp.bfloat16)
-            send_out(stage, 2 + which)
+        send_out(stage, 1, (4, 5, 6, 7, 1, 2, 3, 0))
 
     prepare(0)
     compute(0)
@@ -345,19 +327,13 @@
 
     for stage in range(STAGES):
         for which in range(4):
-
-            def wait_sent(step, carry):
-                in_copy(stage, which, step).wait_send()
-                out_copy(stage, which, step).wait_send()
-                return carry
-
-            def wait_landed(block, carry):
-                slot = outputs[which].at[:, columns(block, stage)]
-                pltpu.make_async_copy(slot, slot, out_recv.at[stage, which, block]).wait()
-                return carry
-
-            lax.fori_loop(1, 8, wait_sent, 0)
-            lax.fori_loop(0, 8, wait_landed, 0)
+            seven = qg.at[stage, 0, pl.ds(0, 7 * T)]
+            pltpu.make_async_copy(seven, seven, in_send.at[stage, which]).wait()
+        for part in range(2):
+            seven = result.at[stage, pl.ds(0, 2), pl.ds(0, 7 * T)]
+            pltpu.make_async_copy(seven, seven, out_send.at[stage, part]).wait()
+            eight = result.at[stage, pl.ds(0, 2)]
+            pltpu.make_async_copy(eight, eight, out_recv.at[stage, part]).wait()
 
 
 def settle(*refs):
@@ -389,14 +365,14 @@
             pltpu.VMEM((STAGES, 2, 2, 3 * T, E), jnp.bfloat16),
             pltpu.VMEM((STAGES, 2, 2, 3 * T, E), jnp.bfloat16),
             pltpu.VMEM((STAGES, 4, 8 * T, E), jnp.bfloat16),
-            dma((STAGES, 4, 8)),
-            dma((STAGES, 4, 8)),
-            dma((STAGES, 2)),
-            dma((STAGES, 2)),
-            dma((STAGES, 2)),
-            dma((STAGES, 2)),
-            dma((STAGES, 4, 8)),
-            dma((STAGES, 4, 8)),
+            dma((STAGES, 4)),
+            dma((STAGES, 4)),
+            dma((STAGES, 2)),
+            dma((STAGES, 2)),
+            dma((STAGES, 2)),
+            dma((STAGES, 2)),
+            dma((STAGES, 2)),
+            dma((STAGES, 2)),
         ],
         compiler_params=pltpu.CompilerParams(
             collective_id=0, has_side_effects=True, vmem_limit_bytes=413 * 2**17

time: 59.9 us -> 56.5 us (0.943)
  Pallas kernels: 59.1 us -> 55.6 us
    pallas_call x1, Pallas kernels: 57.7 us -> 54.2 us  [on_device(): pl.pallas_call(functools.partial(kernel, groups), out_shape=(shape,) * 4,...]
where the time goes in v4:
time: 56.5 us; the launch traced here: 56.2 us
  Pallas kernels  55.6 us (98%)
  between operations  0.64 us (1%)
    pallas_call x1, Pallas kernels, on_device(): pl.pallas_call(functools.partial(kernel, groups), out_shape=(shape,) * 4,...  54.2 us
    pallas_call x1, Pallas kernels, on_device(): pl.pallas_call(settle, out_shape=(shape,) * 4, in_specs=[anywhere] * 4, o...  1.35 us

profile of v4, /device:TPU:8, one launch (start us, length us, event | category | flops | bytes accessed | tf_op | source)
XLA Modules:
  0.0 56.2 jit_solution(4909050846340480398)
XLA Ops:
  0.6 54.2 %shard_map.75 = (bf16[128,2048]{1,0:T(8,128)(2,1)S(1)}, bf16[128,2048]{1,0:T(8,128)(2,1)S(1)}, bf16[128,2048]{1,0:T(8,128)(2,1)S(1)}, bf16[128,2048]{1,0:T(8,128)(2,1)S(1)}) custom-call(bf16[128,2048]{1,0:T(8,128)(2,1)} %q_in.1, bf16[128,2048]{1,0:T(8,128)(2,1)} %k_in.1, bf16[128,2048]{1,0:T(8,128)(2,1)} %v_in.1, bf16[128,2048]{1,0:T(8,128)(2,1)} %g_in.1), custom_call_target="tpu_custom_call" | custom-call | tf_op jit(solution)/shard_map/pallas_call | solution.py:356
  54.9 1.3 %shard_map.76 = (bf16[128,2048]{1,0:T(8,128)(2,1)}, bf16[128,2048]{1,0:T(8,128)(2,1)}, bf16[128,2048]{1,0:T(8,128)(2,1)}, bf16[128,2048]{1,0:T(8,128)(2,1)}) custom-call(bf16[128,2048]{1,0:T(8,128)(2,1)S(1)} %get-tuple-element.8.refs_0_, bf16[128,2048]{1,0:T(8,128)(2,1)S(1)} %get-tuple-element.9.refs_1_, bf16[128,2048]{1,0:T(8,128)(2,1)S(1)} %get-tuple-element.10.refs_2_, ...), custom_call_target="tpu_custom_call" | custom-call | tf_op jit(solution)/shard_map/pallas_call | solution.py:381

commit v5 on v4

--- a/solution.py
+++ b/solution.py
@@ -137,8 +137,6 @@
         pl.semaphore_signal(barrier, inc=1, device_id=(seq, other), device_id_type=MESH)
     pl.semaphore_signal(barrier, inc=1, device_id=nxt, device_id_type=MESH)
     pl.semaphore_signal(barrier, inc=1, device_id=prv, device_id_type=MESH)
-    pl.semaphore_wait(barrier, 9)
-
     inputs = (k_in, v_in, q_in, g_in)
     outputs = (att_out, dq_out, dk_out, dv_out)
     starts = [lax.rem(other + 4 * upper, 8) * (STAGES * E) for other in peers]
@@ -166,8 +164,13 @@
         )
 
     def send_in(stage, which):
-        for step in (1, 2, 3, 4, 5, 6, 7, 0):
+        for step in range(1, 8):
             in_copy(stage, which, step).start()
+
+    for stage in range(STAGES):
+        for which in range(4):
+            in_copy(stage, which, 0).start()
+    pl.semaphore_wait(barrier, 9)
 
     for which in range(3):
         send_in(0, which)
@@ -217,8 +220,9 @@
             device_id_type=MESH,
         )
 
-    def send_out(stage, part, steps):
-        for which in (2 * part, 2 * part + 1):
+    def send_out(stage, arrays, steps):
+        for which in arrays:
+            part = which // 2
             for step in steps:
                 source = result.at[stage, which, rows_of(peers[step])]
                 target = outputs[which].at[:, columns(0, stage)]
@@ -286,11 +290,11 @@
 
             @pl.when(turn == 0)
             def _():
-                send_out(stage, 0, (4, 5, 6, 7))
+                send_out(stage, (0, 1), (4, 5, 6, 7))
 
             @pl.when(turn == 1)
             def _():
-                send_out(stage, 0, (1, 2, 3, 0))
+                send_out(stage, (0, 1), (1, 2, 3, 0))
 
         def next_turn(turn, carry):
             one_quad(turn)
@@ -316,7 +320,7 @@
                 if which == 0:
                     total = total * SCALE
                 result[stage, 2 + which, pl.ds(quad * 512, 512)] = total.astype(jnp.bfloat16)
-        send_out(stage, 1, (4, 5, 6, 7, 1, 2, 3, 0))
+            send_out(stage, (2 + which,), (4, 5, 6, 7, 1, 2, 3, 0))
 
     prepare(0)
     compute(0)
@@ -339,8 +343,9 @@
 def settle(*refs):
     sources, targets, sem = refs[:4], refs[4:8], refs[8]
     copies = [
-        pltpu.make_async_copy(source, target, sem.at[at])
+        pltpu.make_async_copy(source.at[rows], target.at[rows], sem.at[at, half])
         for at, (source, target) in enumerate(zip(sources, targets))
+        for half, rows in enumerate((pl.ds(0, 64), pl.ds(64, 64)))
     ]
     for copy in copies:
         copy.start()
@@ -383,7 +388,7 @@
         out_shape=(shape,) * 4,
         in_specs=[anywhere] * 4,
         out_specs=(anywhere,) * 4,
-        scratch_shapes=[dma((4,))],
+        scratch_shapes=[dma((4, 2))],
         compiler_params=pltpu.CompilerParams(vmem_limit_bytes=2**20),
     )(*moved)
 

time: 56.5 us -> 56.3 us (level)
  no operation moved by 1% of the time
where the time goes in v5:
time: 56.3 us; the launch traced here: 56.1 us
  Pallas kernels  55.4 us (98%)
  between operations  0.64 us (1%)
    pallas_call x1, Pallas kernels, on_device(): pl.pallas_call(functools.partial(kernel, groups), out_shape=(shape,) * 4,...  54.1 us
    pallas_call x1, Pallas kernels, on_device(): pl.pallas_call(settle, out_shape=(shape,) * 4, in_specs=[anywhere] * 4, o...  1.38 us

profile of v5, /device:TPU:8, one launch (start us, length us, event | category | flops | bytes accessed | tf_op | source)
XLA Modules:
  0.0 56.1 jit_solution(3693123774060788478)
XLA Ops:
  0.6 54.1 %shard_map.75 = (bf16[128,2048]{1,0:T(8,128)(2,1)S(1)}, bf16[128,2048]{1,0:T(8,128)(2,1)S(1)}, bf16[128,2048]{1,0:T(8,128)(2,1)S(1)}, bf16[128,2048]{1,0:T(8,128)(2,1)S(1)}) custom-call(bf16[128,2048]{1,0:T(8,128)(2,1)} %q_in.1, bf16[128,2048]{1,0:T(8,128)(2,1)} %k_in.1, bf16[128,2048]{1,0:T(8,128)(2,1)} %v_in.1, bf16[128,2048]{1,0:T(8,128)(2,1)} %g_in.1), custom_call_target="tpu_custom_call" | custom-call | tf_op jit(solution)/shard_map/pallas_call | solution.py:361
  54.7 1.4 %shard_map.76 = (bf16[128,2048]{1,0:T(8,128)(2,1)}, bf16[128,2048]{1,0:T(8,128)(2,1)}, bf16[128,2048]{1,0:T(8,128)(2,1)}, bf16[128,2048]{1,0:T(8,128)(2,1)}) custom-call(bf16[128,2048]{1,0:T(8,128)(2,1)S(1)} %get-tuple-element.8.refs_0_, bf16[128,2048]{1,0:T(8,128)(2,1)S(1)} %get-tuple-element.9.refs_1_, bf16[128,2048]{1,0:T(8,128)(2,1)S(1)} %get-tuple-element.10.refs_2_, ...), custom_call_target="tpu_custom_call" | custom-call | tf_op jit(solution)/shard_map/pallas_call | solution.py:386

commit v6 on v5

--- a/solution.py
+++ b/solution.py
@@ -210,12 +210,12 @@
             device_id_type=MESH,
         )
 
-    def back_copy(stage, side):
+    def back_copy(stage, side, which):
         return pltpu.make_async_remote_copy(
-            src_ref=grad_send.at[stage, side],
-            dst_ref=grad_recv.at[stage, side],
-            send_sem=back_send.at[stage, side],
-            recv_sem=back_recv.at[stage, side],
+            src_ref=grad_send.at[stage, side, which],
+            dst_ref=grad_recv.at[stage, side, which],
+            send_sem=back_send.at[stage, side, which],
+            recv_sem=back_recv.at[stage, side, which],
             device_id=(prv, nxt)[side],
             device_id_type=MESH,
         )
@@ -303,15 +303,16 @@
         lax.fori_loop(0, 2, next_turn, 0)
         grad_send[stage, 0] = acc[stage, :, pl.ds(0, 3 * T)].astype(jnp.bfloat16)
         grad_send[stage, 1] = acc[stage, :, pl.ds(17 * T, 3 * T)].astype(jnp.bfloat16)
-        for side in range(2):
-            back_copy(stage, side).start()
+        for which in range(2):
+            for side in range(2):
+                back_copy(stage, side, which).start()
 
     def finish(stage):
-        for side in range(2):
-            back_copy(stage, side).wait()
-        acc[stage, :, pl.ds(14 * T, 3 * T)] += grad_recv[stage, 0].astype(jnp.float32)
-        acc[stage, :, pl.ds(3 * T, 3 * T)] += grad_recv[stage, 1].astype(jnp.float32)
         for which in range(2):
+            for side, tile in ((0, 14), (1, 3)):
+                back_copy(stage, side, which).wait()
+                received = grad_recv[stage, side, which].astype(jnp.float32)
+                acc[stage, which, pl.ds(tile * T, 3 * T)] += received
             for quad in range(2):
                 fine, coarse = quad_tiles(quad)
                 total = jnp.concatenate([acc[stage, which, rows_of(i)] for i in fine], axis=0)
@@ -374,8 +375,8 @@
             dma((STAGES, 4)),
             dma((STAGES, 2)),
             dma((STAGES, 2)),
-            dma((STAGES, 2)),
-            dma((STAGES, 2)),
+            dma((STAGES, 2, 2)),
+            dma((STAGES, 2, 2)),
             dma((STAGES, 2)),
             dma((STAGES, 2)),
         ],

time: 56.3 us -> 55.6 us (0.988)
  Pallas kernels: 55.4 us -> 54.4 us
    pallas_call x1, Pallas kernels: 54.1 us -> 53.1 us  [on_device(): pl.pallas_call(functools.partial(kernel, groups), out_shape=(shape,) * 4,...]
where the time goes in v6:
time: 55.6 us; the launch traced here: 55.1 us
  Pallas kernels  54.4 us (98%)
  between operations  0.64 us (1%)
    pallas_call x1, Pallas kernels, on_device(): pl.pallas_call(functools.partial(kernel, groups), out_shape=(shape,) * 4,...  53.1 us
    pallas_call x1, Pallas kernels, on_device(): pl.pallas_call(settle, out_shape=(shape,) * 4, in_specs=[anywhere] * 4, o...  1.38 us

profile of v6, /device:TPU:8, one launch (start us, length us, event | category | flops | bytes accessed | tf_op | source)
XLA Modules:
  0.0 55.1 jit_solution(17202240075754900819)
XLA Ops:
  0.6 53.1 %shard_map.75 = (bf16[128,2048]{1,0:T(8,128)(2,1)S(1)}, bf16[128,2048]{1,0:T(8,128)(2,1)S(1)}, bf16[128,2048]{1,0:T(8,128)(2,1)S(1)}, bf16[128,2048]{1,0:T(8,128)(2,1)S(1)}) custom-call(bf16[128,2048]{1,0:T(8,128)(2,1)} %q_in.1, bf16[128,2048]{1,0:T(8,128)(2,1)} %k_in.1, bf16[128,2048]{1,0:T(8,128)(2,1)} %v_in.1, bf16[128,2048]{1,0:T(8,128)(2,1)} %g_in.1), custom_call_target="tpu_custom_call" | custom-call | tf_op jit(solution)/shard_map/pallas_call | solution.py:362
  53.7 1.4 %shard_map.76 = (bf16[128,2048]{1,0:T(8,128)(2,1)}, bf16[128,2048]{1,0:T(8,128)(2,1)}, bf16[128,2048]{1,0:T(8,128)(2,1)}, bf16[128,2048]{1,0:T(8,128)(2,1)}) custom-call(bf16[128,2048]{1,0:T(8,128)(2,1)S(1)} %get-tuple-element.8.refs_0_, bf16[128,2048]{1,0:T(8,128)(2,1)S(1)} %get-tuple-element.9.refs_1_, bf16[128,2048]{1,0:T(8,128)(2,1)S(1)} %get-tuple-element.10.refs_2_, ...), custom_call_target="tpu_custom_call" | custom-call | tf_op jit(solution)/shard_map/pallas_call | solution.py:387
